TPU v7x, 32 devices: a whole 2x2x4 slice. The times are simulated.
32 devices in a mesh: dp: 4 (over x, core), enc: 8 (over z, y).
Axes of the slice: x: 2, y: 2, z: 4, core: 2. Of those that a mesh axis runs over, the one named last changes fastest.
Arguments:
- queries: bfloat16 [8, 1024, 768], P('enc', 'dp'), may hold values from -2.5 to 2.5
- passages: bfloat16 [8, 1536, 768], P('enc', 'dp'), may hold values from -0.25 to 0.25
- pattern: int32 [8, 8, 12], P('enc', 'dp'), may hold values 0 or 1
- positive: int32 [8, 8], P('enc', 'dp'), may hold values from 0 to 11
- owners: int32 [8, 48, 1], P('enc', 'dp'), may hold values from 0 to 7; in each aligned block of 12 rows (0 to 11, 12 to 23, ..., all dimensions but the last counted through in order) at most 2 rows name the same one
- encoder_cache: bfloat16 [8, 2048, 768], P('enc', 'dp'), may hold values from -0.75 to 0.75
- proj_weight: bfloat16 [768, 768], replicated, may hold values from -0.21875 to 0.21875
Outputs:
- losses: float32 [8, 1024], P('enc', 'dp')
- question_derivative_lines: bfloat16 [8, 1024, 768], P('enc', 'dp')
- hidden_grad: bfloat16 [8, 2048, 768], P('enc', 'dp')
- weight_grad: float32 [8, 3072, 768], P('enc', 'dp')
Inputs may be any that keep to these rules, and one draw needn't show every extreme that they name: `owners`: at most 2 of the 12 spans of one device name the same owner, and some device has exactly 2 for one owner.
All inputs are finite; a program needn't handle non-finite values. No bound on the sum of `pattern` on one device may be relied on, other than what follows from the above.
Results may differ from a plain program's by a relative error of at most 0.0051.
Values may be sent and summed in bfloat16 or wider, within the bound.
A program may use at most 64 MiB of HBM per device.

v0:
```python
import jax
import jax.numpy as jnp
from jax import lax
from jax.sharding import PartitionSpec as P

BLOCK = 128
CH = 32
CAP = 2


normalizer_coolness_factor = 0.05


def block_scores(question_vector_lines, document_vector_lines):
    match_energies = (
        jnp.dot(question_vector_lines, document_vector_lines.T, preferred_element_type=jnp.float32)
        / normalizer_coolness_factor
    )
    return match_energies.reshape(
        question_vector_lines.shape[0] // BLOCK,
        BLOCK,
        document_vector_lines.shape[0] // BLOCK,
        BLOCK,
    )


def block_masks(pattern_rows, positive_rows, first_block, block_count):
    columns = lax.dynamic_slice_in_dim(pattern_rows, first_block, block_count, 1)
    block_ids = first_block + jnp.arange(block_count, dtype=jnp.int32)
    target_block = positive_rows[:, None] == block_ids[None, :]
    allowed = (columns == 1) | target_block
    diagonal = jnp.eye(BLOCK, dtype=jnp.bool_)
    allowed_full = allowed[:, None, :, None]
    target_hit = target_block[:, None, :, None] & diagonal[None, :, None, :]
    return (allowed_full, target_hit)


def partial_update(match_energies, allowed_full, target_hit, row_max):
    masked = jnp.where(allowed_full, match_energies, -jnp.inf)
    local_max = jnp.max(masked, axis=(2, 3)).reshape(-1)
    new_max = jnp.maximum(row_max, local_max)
    shifted = match_energies - new_max.reshape(match_energies.shape[0], BLOCK, 1, 1)
    exp_terms = jnp.where(allowed_full, jnp.exp(shifted), 0.0)
    new_sum = jnp.sum(exp_terms, axis=(2, 3)).reshape(-1)
    picked = jnp.where(target_hit, match_energies, 0.0)
    new_positive = jnp.sum(picked, axis=(2, 3)).reshape(-1)
    return (new_max, new_sum, new_positive)


def softmax_terms(match_energies, allowed_full, target_hit, log_total):
    shifted = match_energies - log_total.reshape(match_energies.shape[0], BLOCK, 1, 1)
    probability = jnp.where(allowed_full, jnp.exp(shifted), 0.0)
    centered_match_energies = probability - target_hit.astype(jnp.float32)
    return centered_match_energies.astype(jnp.bfloat16).reshape(
        match_energies.shape[0] * BLOCK, match_energies.shape[2] * BLOCK
    )


def local_softmax(question_vector_lines, gathered, pattern_rows, positive_rows, start_max):
    match_energies = block_scores(question_vector_lines, gathered)
    allowed_full, target_hit = block_masks(
        pattern_rows, positive_rows, 0, gathered.shape[0] // BLOCK
    )
    row_max, row_sum, positive_score = partial_update(
        match_energies, allowed_full, target_hit, start_max
    )
    log_total = row_max + jnp.log(row_sum)
    centered_match_energies = softmax_terms(match_energies, allowed_full, target_hit, log_total)
    question_accrued_mass = jnp.dot(
        centered_match_energies, gathered, preferred_element_type=jnp.float32
    )
    return (log_total, positive_score, centered_match_energies, question_accrued_mass)


def body(queries, passages, pattern, positive, owners, encoder_cache, proj_weight):
    question_vector_lines = queries[0]
    document_vector_lines = passages[0]
    pattern_rows = pattern[0]
    positive_rows = positive[0]
    query_count = question_vector_lines.shape[0]
    block_count = document_vector_lines.shape[0] // BLOCK
    first_block = lax.axis_index("dp") * block_count
    start_max = jnp.full((query_count,), -1e30, jnp.float32)
    gathered = lax.all_gather(document_vector_lines, "dp", axis=0, tiled=True)
    log_total, positive_score, centered_match_energies, question_accrued_mass = local_softmax(
        question_vector_lines, gathered, pattern_rows, positive_rows, start_max
    )
    group_rows = (
        lax.all_gather(question_vector_lines.astype(jnp.float32), "dp", axis=0, tiled=True),
        lax.all_gather(pattern_rows, "dp", axis=0, tiled=True),
        lax.all_gather(positive_rows, "dp", axis=0, tiled=True),
        lax.all_gather(log_total, "dp", axis=0, tiled=True),
    )
    all_queries = group_rows[0].astype(jnp.bfloat16)
    all_scores = block_scores(all_queries, document_vector_lines)
    all_allowed, all_target = block_masks(group_rows[1], group_rows[2], first_block, block_count)
    all_adjusted = softmax_terms(all_scores, all_allowed, all_target, group_rows[3])
    document_accrued_mass = jnp.dot(all_adjusted.T, all_queries, preferred_element_type=jnp.float32)
    losses = (log_total - positive_score)[None]
    question_derivative_lines = (question_accrued_mass / normalizer_coolness_factor).astype(
        jnp.bfloat16
    )[None]
    document_derivative_lines = (document_accrued_mass / normalizer_coolness_factor).astype(
        jnp.bfloat16
    )
    owner_count = lax.axis_size("enc")
    span_count = document_derivative_lines.shape[0] // CH
    feature_width = document_derivative_lines.shape[1]
    owner_ids = owners[0, :, 0]
    owner_hit = (owner_ids[:, None] == jnp.arange(owner_count, dtype=jnp.int32)[None, :]).astype(
        jnp.int32
    )
    earlier = jnp.cumsum(owner_hit, axis=0) - owner_hit
    owner_rank = jnp.sum(earlier * owner_hit, axis=1)
    slot_index = owner_ids * CAP + owner_rank
    selector = (
        jnp.arange(owner_count * CAP, dtype=jnp.int32)[:, None] == slot_index[None, :]
    ).astype(jnp.bfloat16)
    outgoing = jnp.dot(
        selector,
        document_derivative_lines.reshape(span_count, CH * feature_width),
        preferred_element_type=jnp.float32,
    ).astype(jnp.bfloat16)
    outgoing = outgoing.reshape(owner_count * CAP * CH, feature_width)
    received = lax.all_to_all(outgoing, "enc", split_axis=0, concat_axis=0, tiled=True)
    hidden_grad = jnp.dot(received, proj_weight.T, preferred_element_type=jnp.float32).astype(
        jnp.bfloat16
    )
    weight_grad = jnp.dot(encoder_cache[0].T, received, preferred_element_type=jnp.float32)
    return (losses, question_derivative_lines, hidden_grad[None], weight_grad[None])


def solution(mesh):
    placed = (
        P("enc", "dp", None),
        P("enc", "dp", None),
        P("enc", "dp", None),
        P("enc", "dp"),
        P("enc", "dp", None),
        P("enc", "dp", None),
        P(),
    )
    return jax.shard_map(
        body,
        mesh=mesh,
        in_specs=placed,
        out_specs=(
            P("enc", "dp"),
            P("enc", "dp", None),
            P("enc", "dp", None),
            P("enc", "dp", None),
        ),
        check_vma=False,
    )
```

profile of v0, /device:TPU:0, one launch (start us, length us, event | category | flops | bytes accessed | tf_op | source)
XLA Modules:
  0.0 105.9 jit_solution(1091135076260854514)
XLA Ops:
  7.2 0.7 all-gather.9.cloned.1.call-update
  8.0 0.7 all-gather.7.cloned.1.call-update
  8.7 6.3 %all-gather.1 = s32[1,8,12]{2,0,1:T(1,128)S(1)} all-gather(s32[1,2,12]{2,0,1:T(1,128)} %bitcast.94), channel_id=3, replica_groups=mesh['dp'=4,'enc'=8] {'dp'}, dimensions={1}, use_global_device_ids=true | all-gather | bytes 480 | tf_op jit(solution)/shard_map/all_gather | solution.py:90
  15.1 1.2 %dynamic-slice.1 = u32[1]{0:T(128)} dynamic-slice(u32[32]{0:T(128)} %constant.44, u32[]{:T(128)S(6)} %add.40), dynamic_slice_sizes={1} | dynamic-slice | bytes 12
  17.0 0.8 bitcast_dynamic-update-slice_fusion
  17.9 5.4 %all-reduce = s32[8]{0:T(128)S(1)} all-reduce(s32[8]{0:T(128)S(1)} %bitcast_dynamic-update-slice_fusion), channel_id=4, replica_groups=mesh['dp'=4,'enc'=8] {'dp'}, use_global_device_ids=true, to_apply=%add | all-reduce | flops 8 | bytes 64
  23.4 0.2 and_convert_fusion
  23.6 0.3 copy.60
  23.9 1.6 %copy.40 = f32[1024,384]{1,0:T(8,128)} copy(f32[1024,384]{0,1:T(8,128)S(1)} %bitcast.83) | data formatting | bytes 3145728 | tf_op jit(solution)/shard_map/convert_element_type | solution.py:53
  25.6 0.2 broadcast_in_dim.71
  25.7 0.2 copy.61
  25.9 1.2 %copy.39 = pred[1024,384]{1,0:T(32,128)(4,1)} copy(pred[1024,384]{0,1:T(8,128)(4,1)S(1)} %bitcast.90) | data formatting | bytes 786432 | tf_op jit(solution)/shard_map/jit(_where)/broadcast_in_dim | solution.py:52
  27.2 0.2 reduce_window_sum.11
  27.5 0.3 broadcast_and_fusion
  27.8 8.7 %all-gather.9.cloned.1.call-done = bf16[1,1536,768]{2,1,0:T(8,128)(2,1)} async-done(((bf16[1,384,768]{2,1,0:T(8,128)(2,1)}), bf16[1,1536,768]{2,1,0:T(8,128)(2,1)}) %all-gather.9.cloned.1.call-update) | async-done | bytes 2359312 | tf_op jit(solution)/shard_map/all_gather | solution.py:84
  36.5 0.2 broadcast_in_dim.65
  36.7 2.8 %select_reduce_fusion.2 = (f32[256]{0:T(256)S(1)}, f32[256,1536]{1,0:T(8,128)S(1)}) fusion(pred[32,8,12,128]{3,2,1,0:T(8,128)(4,1)S(1)} %bitcast.86, bf16[1,1536,768]{2,1,0:T(8,128)(2,1)} %all-gather.9.cloned.1.call-done, bf16[1,256,768]{2,1,0:T(8,128)(2,1)S(1)} %copy-done.5), kind=kOutput, calls=%fused_computation.11 | convolution fusion | flops 605159168 | bytes 4719616 | tf_op jit(solution)/shard_map/dot_general | solution.py:16
  39.6 0.7 select_reduce_fusion
  40.3 0.4 copy-done.3
  40.7 0.6 fusion.31
  41.2 5.1 %all-gather.3 = f32[4,1,256]{2,1,0:T(1,128)S(1)} all-gather(f32[1,1,256]{2,1,0:T(1,128)S(1)} %bitcast.92), channel_id=1, replica_groups=mesh['dp'=4,'enc'=8] {'dp'}, dimensions={0}, use_global_device_ids=true | all-gather | bytes 5120 | tf_op jit(solution)/shard_map/all_gather | solution.py:92
  46.3 11.4 %all-gather.7.cloned.1.call-done = bf16[1024,768]{1,0:T(8,128)(2,1)} async-done(((bf16[256,768]{1,0:T(8,128)(2,1)}), bf16[1024,768]{1,0:T(8,128)(2,1)}) %all-gather.7.cloned.1.call-update) | async-done | bytes 1572880 | tf_op jit(solution)/shard_map/all_gather | solution.py:89
  57.7 5.3 %fusion.3 = bf16[384,768]{1,0:T(8,128)(2,1)} fusion(f32[1024,384]{1,0:T(8,128)} %copy.40, pred[1024,384]{1,0:T(32,128)(4,1)S(1)} %copy-done.6, bf16[1024,768]{1,0:T(8,128)(2,1)} %all-gather.7.cloned.1.call-done, f32[1024]{0:T(1024)S(1)} %bitcast.93, bf16[1,384,768]{2,1,0:T(8,128)(2,1)S(1)} %copy-done.4), kind=kOutput, calls=%fused_computation.16 | convolution fusion | flops 1210515456 | bytes 4722688 | tf_op jit(solution)/shard_map/dot_general | solution.py:98
  63.0 1.5 %reshape.192 = bf16[12,24576]{1,0:T(8,128)(2,1)S(1)} reshape(bf16[384,768]{1,0:T(8,128)(2,1)} %fusion.3) | data formatting | bytes 1179648 | tf_op jit(solution)/shard_map/reshape | solution.py:121
  64.5 0.3 convolution_convert_fusion
  64.8 1.2 %all_to_all.8 = bf16[8,64,768]{2,1,0:T(8,128)(2,1)} reshape(bf16[16,24576]{1,0:T(8,128)(2,1)S(1)} %convolution_convert_fusion) | data formatting | bytes 1572864 | tf_op jit(solution)/shard_map/all_to_all | solution.py:125
  66.1 5.5 %all-to-all-start = ((bf16[8,64,768]{2,1,0:T(8,128)(2,1)}), bf16[8,64,768]{2,1,0:T(8,128)(2,1)}, u32[]{:S(2)}, u32[]{:S(2)}) async-start(bf16[8,64,768]{2,1,0:T(8,128)(2,1)} %all_to_all.8), calls=%async_computation | async-start | bytes 1572864 | tf_op jit(solution)/shard_map/all_to_all | solution.py:125
  71.6 4.0 %fusion.11 = bf16[1,256,768]{2,1,0:T(8,128)(2,1)} fusion(bf16[1,1536,768]{2,1,0:T(8,128)(2,1)} %all-gather.9.cloned.1.call-done, f32[256,1536]{1,0:T(8,128)} %copy-done.3, pred[32,8,12,128]{3,2,1,0:T(8,128)(4,1)S(1)} %bitcast.85, f32[256]{0:T(256)S(1)} %get-tuple-element.33, pred[32,8,12,128]{3,2,1,0:T(8,128)(4,1)S(1)} %bitcast.88), kind=kOutput, calls=%fused_computation.20 | convolution fusion | flops 606339072 | bytes 5112832 | tf_op jit(solution)/shard_map/dot_general | solution.py:69
  75.6 16.6 %all-to-all-done = bf16[8,64,768]{2,1,0:T(8,128)(2,1)} async-done(((bf16[8,64,768]{2,1,0:T(8,128)(2,1)}), bf16[8,64,768]{2,1,0:T(8,128)(2,1)}, u32[]{:S(2)}, u32[]{:S(2)}) %all-to-all-start) | async-done | bytes 786464 | tf_op jit(solution)/shard_map/all_to_all | solution.py:125
  92.2 2.9 %fusion.4 = bf16[1,512,768]{2,1,0:T(8,128)(2,1)} fusion(bf16[512,768]{1,0:T(8,128)(2,1)} %bitcast.12, bf16[768,768]{1,0:T(8,128)(2,1)S(1)} %copy-done), kind=kOutput, calls=%fused_computation.17 | convolution fusion | flops 604372992 | bytes 2752512 | tf_op jit(solution)/shard_map/dot_general | solution.py:126
  95.1 1.9 %convolution_bitcast_fusion = f32[1,768,768]{1,2,0:T(8,128)S(1)} fusion(bf16[512,768]{1,0:T(8,128)(2,1)} %bitcast.12, bf16[1,512,768]{2,1,0:T(8,128)(2,1)S(1)} %copy-done.10), kind=kOutput, calls=%fused_computation.5 | convolution fusion | flops 603979776 | bytes 3932160 | tf_op jit(solution)/shard_map/dot_general | solution.py:129
  97.1 2.0 %copy.41 = f32[1,768,768]{2,1,0:T(8,128)} copy(f32[1,768,768]{1,2,0:T(8,128)S(1)} %convolution_bitcast_fusion) | data formatting | bytes 4718592
  (36 shorter events, 0.6 us)
Async XLA Ops:
  7.2 85.1 %copy-start = (bf16[768,768]{1,0:T(8,128)(2,1)S(1)}, bf16[768,768]{1,0:T(8,128)(2,1)}, u32[]{:S(2)}) copy-start(bf16[768,768]{1,0:T(8,128)(2,1)} %param.13) | copy-start | bytes 3538948
  7.2 29.3 %all-gather.9.cloned.1.call-start = ((), (), s32[]{:S(2)}) async-start(), calls=%async_computation.2 | async-start | bytes 2949120 | tf_op jit(solution)/shard_map/all_gather | solution.py:84
  7.9 49.8 %all-gather.7.cloned.1.call-start = ((), (), s32[]{:S(2)}) async-start(), calls=%async_computation.1 | async-start | bytes 1966080 | tf_op jit(solution)/shard_map/all_gather | solution.py:89
  25.5 1.6 %copy-start.8 = (s32[1,12,1]{1,2,0:T(1,128)S(1)}, s32[1,12,1]{1,2,0:T(1,128)}, u32[]{:S(2)}) copy-start(s32[1,12,1]{1,2,0:T(1,128)} %param.11) | copy-start | bytes 148
  25.5 1.8 %copy-start.7 = (s32[1,2,12]{2,1,0:T(2,128)S(1)}, s32[1,2,12]{2,1,0:T(2,128)}, u32[]{:S(2)}) copy-start(s32[1,2,12]{2,1,0:T(2,128)} %param.9) | copy-start | bytes 292
  25.5 1.8 %copy-start.9 = (s32[1,2]{1,0:T(1,128)S(1)}, s32[1,2]{1,0:T(1,128)}, u32[]{:S(2)}) copy-start(s32[1,2]{1,0:T(1,128)} %param.10) | copy-start | bytes 28
  25.6 11.2 %copy-start.5 = (bf16[1,256,768]{2,1,0:T(8,128)(2,1)S(1)}, bf16[1,256,768]{2,1,0:T(8,128)(2,1)}, u32[]{:S(2)}) copy-start(bf16[1,256,768]{2,1,0:T(8,128)(2,1)} %param.7) | copy-start | bytes 1179652
  36.7 2.9 %copy-start.1 = (pred[2,128,12,128]{3,2,1,0:T(8,128)(4,1)}, pred[2,128,12,128]{3,2,1,0:T(8,128)(4,1)S(1)}, u32[]{:S(2)}) copy-start(pred[2,128,12,128]{3,2,1,0:T(8,128)(4,1)S(1)} %broadcast_in_dim.65) | copy-start | bytes 1179652
  39.5 1.1 %copy-start.3 = (f32[256,1536]{1,0:T(8,128)}, f32[256,1536]{1,0:T(8,128)S(1)}, u32[]{:S(2)}) copy-start(f32[256,1536]{1,0:T(8,128)S(1)} %get-tuple-element.37) | copy-start | bytes 4718596
  39.5 18.2 %copy-start.4 = (bf16[1,384,768]{2,1,0:T(8,128)(2,1)S(1)}, bf16[1,384,768]{2,1,0:T(8,128)(2,1)}, u32[]{:S(2)}) copy-start(bf16[1,384,768]{2,1,0:T(8,128)(2,1)} %param.8) | copy-start | bytes 1769476
  39.5 18.2 %copy-start.6 = (pred[1024,384]{1,0:T(32,128)(4,1)S(1)}, pred[1024,384]{1,0:T(32,128)(4,1)}, u32[]{:S(2)}) copy-start(pred[1024,384]{1,0:T(32,128)(4,1)} %copy.39) | copy-start | bytes 1179652
  64.8 6.8 %copy-start.2 = (pred[2,128,12,128]{3,2,1,0:T(8,128)(4,1)S(1)}, pred[2,128,12,128]{3,2,1,0:T(8,128)(4,1)}, u32[]{:S(2)}) copy-start(pred[2,128,12,128]{3,2,1,0:T(8,128)(4,1)} %copy-done.1) | copy-start | bytes 1179652
  66.1 26.2 %all-to-all-start = ((bf16[8,64,768]{2,1,0:T(8,128)(2,1)}), bf16[8,64,768]{2,1,0:T(8,128)(2,1)}, u32[]{:S(2)}, u32[]{:S(2)}) async-start(bf16[8,64,768]{2,1,0:T(8,128)(2,1)} %all_to_all.8), calls=%async_computation | async-start | bytes 1572864 | tf_op jit(solution)/shard_map/all_to_all | solution.py:125
  92.2 2.9 %copy-start.10 = (bf16[1,512,768]{2,1,0:T(8,128)(2,1)S(1)}, bf16[1,512,768]{2,1,0:T(8,128)(2,1)}, u32[]{:S(2)}) copy-start(bf16[1,512,768]{2,1,0:T(8,128)(2,1)} %param.12) | copy-start | bytes 2359300
Sparse Core Ops, SparseCore 0:
  9.6 26.8 all-gather.8
  38.0 19.6 all-gather.6
where the time goes:
time: 106 us
  waiting for transfers between devices  38.1 us (36%)
  matrix products  17.3 us (16%)
  blocking collectives  16.7 us (16%)
  between operations  14.9 us (14%)
  local copies, waits for them, and re-layouts  11.1 us (10%)
  starting transfers between devices  5.59 us (5%)
  other arithmetic  2.15 us (2%)
    all_to_all x1, waiting for transfers between devices, body(): lax.all_to_all(outgoing, 'enc', split_axis=0, concat_axis=0, tiled=True)  16.6 us
    all_gather x1, waiting for transfers between devices, body(): lax.all_gather(question_vector_lines.astype(jnp.float32), 'dp', axis=0, t...  11.4 us
    all_gather x1, waiting for transfers between devices, body(): gathered = lax.all_gather(document_vector_lines, 'dp', axis=0, tiled=True)  8.7 us
    all_gather x1, blocking collectives, body(): lax.all_gather(pattern_rows, 'dp', axis=0, tiled=True)  6.25 us
    all_to_all x1, starting transfers between devices, body(): lax.all_to_all(outgoing, 'enc', split_axis=0, concat_axis=0, tiled=True)  5.52 us
    unnamed x1, blocking collectives  5.42 us
    dot_general x1, matrix products, body(): jnp.dot(all_adjusted.T, all_queries, preferred_element_type=jnp.float32)  5.25 us
    all_gather x1, blocking collectives, body(): lax.all_gather(log_total, 'dp', axis=0, tiled=True)  5.06 us
  transfers between devices with their start and end apart: 3, of which 3 were waited for; matrix products, arithmetic and copies ran while one was open for 14% of the time, Pallas kernels for 0%

commit v1 on v0

v1 whole, which is shorter than its diff:
```python
import functools

import jax
import jax.numpy as jnp
from jax import lax
from jax.experimental import pallas as pl
from jax.experimental.pallas import tpu as pltpu
from jax.sharding import PartitionSpec as P

BLOCK = 128
CH = 32
CAP = 2
CHUNKS = 4
NEVER = -1e30
INVERSE_COOLNESS = 20.0


def remote(src, dst, send_sem, recv_sem, target):
    return pltpu.make_async_remote_copy(
        src_ref=src,
        dst_ref=dst,
        send_sem=send_sem,
        recv_sem=recv_sem,
        device_id=target,
        device_id_type=pl.DeviceIdType.MESH,
    )


def rows_at(index, count):
    return pl.ds(pl.multiple_of(index * count, count), count)


def group_kernel(
    n_dp, n_enc, q_ref, p_ref, pattern_ref, positive_ref, owners_ref,
    losses_ref, dq_ref, received_ref,
    q_all, p_own, code_out, code_all, s_all, adj, stat_all, dp_sum, outgoing,
    dqs_out, dqs_in, dq_own, dqx_out, dqx_in, select,
    load_sem, qs_sem, qx_send, qx_recv, qf_send, qf_recv, code_send, code_recv,
    stat_send, stat_recv, dqs_send, dqs_recv, dqx_send, dqx_recv, a2a_send, a2a_recv,
):
    me = lax.axis_index("dp")
    my_owner = lax.axis_index("enc")
    n_pair = n_dp // 2
    pair, core = me // 2, me % 2
    sibling = pair * 2 + 1 - core
    rows, width = q_ref.shape
    passage_rows = p_ref.shape[0]
    blocks = passage_rows // BLOCK
    query_blocks = rows // BLOCK
    span_count = passage_rows // CH
    part = rows // CHUNKS
    slot_rows = CAP * CH

    def dp_target(index):
        return {"dp": index}

    barrier = pltpu.get_barrier_semaphore()
    for k in range(1, n_dp):
        pl.semaphore_signal(
            barrier, inc=1, device_id=dp_target((me + k) % n_dp),
            device_id_type=pl.DeviceIdType.MESH,
        )
    for k in range(1, n_enc):
        pl.semaphore_signal(
            barrier, inc=1, device_id={"enc": (my_owner + k) % n_enc},
            device_id_type=pl.DeviceIdType.MESH,
        )
    load_q = pltpu.make_async_copy(q_ref, q_all.at[rows_at(me, rows)], load_sem.at[0])
    load_p = pltpu.make_async_copy(p_ref, p_own, load_sem.at[1])
    load_q.start()
    load_p.start()
    pl.semaphore_wait(barrier, n_dp + n_enc - 2)

    def chunk(source, h):
        return pl.ds(pl.multiple_of(source * rows + h * part, part), part)

    def query_send(t, h):
        target = ((pair + t) % n_pair) * 2 + core
        return remote(
            q_ref.at[pl.ds(h * part, part)], q_all.at[chunk(me, h)],
            qx_send.at[t, h], qx_recv.at[t, h], dp_target(target),
        )

    def query_arrival(t, h):
        source = ((pair - t + n_pair) % n_pair) * 2 + core
        view = q_all.at[chunk(source, h)]
        return remote(view, view, qx_send.at[t, h], qx_recv.at[t, h], dp_target(source))

    def query_forward(t, h, owner_core):
        source = ((pair - t + n_pair) % n_pair) * 2 + owner_core
        view = q_all.at[chunk(source, h)]
        return remote(view, view, qf_send.at[t, h], qf_recv.at[t, h], dp_target(sibling))

    for h in range(CHUNKS):
        for t in range(1, n_pair):
            query_send(t, h).start()
    to_sibling = remote(
        q_ref, q_all.at[rows_at(me, rows)], qs_sem.at[0], qs_sem.at[1], dp_target(sibling)
    )
    to_sibling.start()

    code_out[...] = jnp.zeros_like(code_out)
    for b in range(query_blocks):
        for j in range(n_dp * blocks):
            hit = (positive_ref[0, b] == j).astype(jnp.int32)
            seen = (pattern_ref[0, b, j] == 1).astype(jnp.int32)
            value = jnp.maximum(2 * hit, seen).astype(jnp.float32)
            code_out[j // blocks, j % blocks : j % blocks + 1, b * BLOCK : (b + 1) * BLOCK] = (
                jnp.full((1, BLOCK), value, jnp.float32)
            )
    code_all[me] = code_out[me]

    def code_copy(k):
        target = (me + k) % n_dp
        return remote(
            code_out.at[target], code_all.at[me], code_send.at[k], code_recv.at[k],
            dp_target(target),
        )

    for k in range(1, n_dp):
        code_copy(k).start()

    def select_spans(owner, carry):
        seen = jnp.int32(0)
        found = [jnp.int32(-1)] * CAP
        for c in range(span_count):
            hit = (owners_ref[0, c, 0] == owner).astype(jnp.int32)
            for r in range(CAP):
                found[r] = found[r] + (c + 1) * hit * (seen == r).astype(jnp.int32)
            seen = seen + hit
        line = lax.broadcasted_iota(jnp.int32, (CH, passage_rows), 0)
        column = lax.broadcasted_iota(jnp.int32, (CH, passage_rows), 1)
        for r in range(CAP):
            chosen = (column == line + found[r] * CH).astype(jnp.float32)
            select[rows_at(owner * CAP + r, CH), :] = chosen.astype(jnp.bfloat16)
        return carry

    lax.fori_loop(0, n_enc, select_spans, 0)

    on_diagonal = (
        lax.broadcasted_iota(jnp.int32, (BLOCK, rows), 0)
        == lax.broadcasted_iota(jnp.int32, (BLOCK, rows), 1) % BLOCK
    )

    def score(source):
        columns = rows_at(source, rows)
        scores = lax.dot_general(
            p_own[...], q_all[columns, :], (((1,), (1,)), ((), ())),
            preferred_element_type=jnp.float32,
        ) * INVERSE_COOLNESS
        top = jnp.full((1, rows), NEVER, jnp.float32)
        picked = jnp.zeros((1, rows), jnp.float32)
        masked = []
        for j in range(blocks):
            block = scores[j * BLOCK : (j + 1) * BLOCK, :]
            code = code_all[source, j : j + 1, :]
            block_masked = jnp.where(code > 0.5, block, NEVER)
            s_all[j * BLOCK : (j + 1) * BLOCK, columns] = block_masked
            masked.append(block_masked)
            top = jnp.maximum(top, jnp.max(block_masked, axis=0, keepdims=True))
            hit = on_diagonal & (code > 1.5)
            picked = picked + jnp.sum(jnp.where(hit, block, 0.0), axis=0, keepdims=True)
        shift = jnp.where(top > 0.5 * NEVER, top, 0.0)
        total = jnp.zeros((1, rows), jnp.float32)
        for j in range(blocks):
            total = total + jnp.sum(jnp.exp(masked[j] - shift), axis=0, keepdims=True)
        stat_all[me, 0:1, columns] = jnp.where(
            total > 0.0, shift + jnp.log(jnp.maximum(total, 1e-30)), NEVER
        )
        stat_all[me, 1:2, columns] = picked

    load_q.wait()
    load_p.wait()

    def code_wait(k):
        source = (me - k + n_dp) % n_dp
        remote(
            code_out.at[0], code_all.at[source], code_send.at[k], code_recv.at[k],
            dp_target(source),
        ).wait_recv()

    score(me)
    remote(
        q_ref, q_all.at[rows_at(sibling, rows)], qs_sem.at[0], qs_sem.at[1], dp_target(sibling)
    ).wait_recv()
    for k in range(1, n_dp):
        code_wait(k)
    score(sibling)

    def take_and_forward(t, carry):
        for h in range(CHUNKS):
            query_arrival(t, h).wait_recv()
            query_forward(t, h, core).start()
        score(((pair - t + n_pair) % n_pair) * 2 + core)
        return carry

    lax.fori_loop(1, n_pair, take_and_forward, 0)

    def take_forwarded(t, carry):
        for h in range(CHUNKS):
            query_forward(t, h, 1 - core).wait_recv()
        score(((pair - t + n_pair) % n_pair) * 2 + 1 - core)
        return carry

    lax.fori_loop(1, n_pair, take_forwarded, 0)

    def stat_copy(k, source, target):
        view = stat_all.at[source]
        return remote(view, view, stat_send.at[k], stat_recv.at[k], dp_target(target))

    for k in range(1, n_dp):
        stat_copy(k, me, (me + k) % n_dp).start()
    for k in range(1, n_dp):
        stat_copy(k, (me - k + n_dp) % n_dp, me).wait_recv()

    def adjust(source, carry):
        columns = rows_at(source, rows)
        parts = [stat_all[d, 0:1, columns] for d in range(n_dp)]
        top = functools.reduce(jnp.maximum, parts)
        total = functools.reduce(jnp.add, [jnp.exp(x - top) for x in parts])
        log_total = top + jnp.log(total)
        for j in range(blocks):
            lines = slice(j * BLOCK, (j + 1) * BLOCK)
            hit = on_diagonal & (code_all[source, j : j + 1, :] > 1.5)
            probability = jnp.exp(s_all[lines, columns] - log_total)
            adj[lines, columns] = (probability - jnp.where(hit, 1.0, 0.0)).astype(jnp.bfloat16)
        return carry

    lax.fori_loop(0, n_dp, adjust, 0)

    depth = min(n_dp * rows, 1024)
    if depth == n_dp * rows:
        for n in range(0, width, 256):
            lanes = slice(n, n + 256)
            dp_sum[:, lanes] = jnp.dot(
                adj[...], q_all[:, lanes], preferred_element_type=jnp.float32
            )
    else:
        dp_sum[...] = jnp.zeros_like(dp_sum)

        def add_group(g, carry):
            inner = rows_at(g, depth)
            for n in range(0, width, 256):
                lanes = slice(n, n + 256)
                dp_sum[:, lanes] += jnp.dot(
                    adj[:, inner], q_all[inner, lanes], preferred_element_type=jnp.float32
                )
            return carry

        lax.fori_loop(0, n_dp * rows // depth, add_group, 0)

    for n in range(0, width, 256):
        lanes = slice(n, n + 256)
        grad = (dp_sum[:, lanes] * INVERSE_COOLNESS).astype(jnp.bfloat16)
        outgoing[:, lanes] = jnp.dot(
            select[...], grad, preferred_element_type=jnp.float32
        ).astype(jnp.bfloat16)

    def span_copy(k):
        owner = (my_owner + k) % n_enc
        return remote(
            outgoing.at[rows_at(owner, slot_rows)], received_ref.at[rows_at(my_owner, slot_rows)],
            a2a_send.at[k], a2a_recv.at[k], {"enc": owner},
        )

    def send_spans(k, carry):
        span_copy(k).start()
        return carry

    lax.fori_loop(1, n_enc, send_spans, 0)
    keep = pltpu.make_async_copy(
        outgoing.at[rows_at(my_owner, slot_rows)],
        received_ref.at[rows_at(my_owner, slot_rows)],
        load_sem.at[2],
    )
    keep.start()

    def partial(source):
        return lax.dot_general(
            adj[:, rows_at(source, rows)], p_own[...], (((0,), (0,)), ((), ())),
            preferred_element_type=jnp.float32,
        )

    def dqs_copy(t):
        return remote(
            dqs_out.at[t], dqs_in.at[t], dqs_send.at[t], dqs_recv.at[t], dp_target(sibling)
        )

    def dqx_copy(t):
        target = ((pair + t) % n_pair) * 2 + core
        return remote(
            dqx_out.at[t], dqx_in.at[t], dqx_send.at[t], dqx_recv.at[t], dp_target(target)
        )

    def sibling_share(t, carry):
        target = ((pair + t) % n_pair) * 2
        dqs_out[t] = partial(target + 1 - core).astype(jnp.bfloat16)
        dqs_copy(t).start()
        return carry

    def chip_share(t, carry):
        target = ((pair + t) % n_pair) * 2
        dq_own[...] = partial(target + core)
        dqs_copy(t).wait_recv()
        dqx_out[t] = (dq_own[...] + dqs_in[t].astype(jnp.float32)).astype(jnp.bfloat16)
        dqx_copy(t).start()
        return carry

    lax.fori_loop(1, n_pair, sibling_share, 0)
    lax.fori_loop(1, n_pair, chip_share, 0)
    sibling_share(0, 0)
    dq_own[...] = partial(me)
    dqs_copy(0).wait_recv()
    dq_own[...] += dqs_in[0].astype(jnp.float32)

    own = rows_at(me, rows)
    parts = [stat_all[d, 0:1, own] for d in range(n_dp)]
    top = functools.reduce(jnp.maximum, parts)
    total = functools.reduce(jnp.add, [jnp.exp(x - top) for x in parts])
    picked = functools.reduce(jnp.add, [stat_all[d, 1:2, own] for d in range(n_dp)])
    losses_ref[...] = top + jnp.log(total) - picked

    def add_chip(t, carry):
        dqx_copy(t).wait_recv()
        dq_own[...] += dqx_in[t].astype(jnp.float32)
        return carry

    lax.fori_loop(1, n_pair, add_chip, 0)
    dq_ref[...] = (dq_own[...] * INVERSE_COOLNESS).astype(jnp.bfloat16)

    to_sibling.wait_send()
    for t in range(1, n_pair):
        for h in range(CHUNKS):
            query_send(t, h).wait_send()
            query_forward(t, h, core).wait_send()
    for k in range(1, n_dp):
        code_copy(k).wait_send()
        stat_copy(k, me, (me + k) % n_dp).wait_send()
    for t in range(n_pair):
        dqs_copy(t).wait_send()
        if t:
            dqx_copy(t).wait_send()
    for k in range(1, n_enc):
        span_copy(k).wait_send()
    for k in range(1, n_enc):
        source = (my_owner - k + n_enc) % n_enc
        remote(
            outgoing.at[rows_at(source, slot_rows)], received_ref.at[rows_at(source, slot_rows)],
            a2a_send.at[k], a2a_recv.at[k], {"enc": source},
        ).wait_recv()
    keep.wait()


def body(n_dp, n_enc, queries, passages, pattern, positive, owners, encoder_cache, proj_weight):
    rows, width = queries.shape[1:]
    passage_rows = passages.shape[1]
    blocks = passage_rows // BLOCK
    code_rows = -(-blocks // 8) * 8
    n_pair = n_dp // 2
    total_rows = n_dp * rows
    slots = n_enc * CAP * CH
    bf16, f32 = jnp.bfloat16, jnp.float32
    dma = pltpu.SemaphoreType.DMA
    smem = pl.BlockSpec(memory_space=pltpu.SMEM)
    vmem = pl.BlockSpec(memory_space=pltpu.VMEM)
    hbm = pl.BlockSpec(memory_space=pl.ANY)
    losses, dq, received = pl.pallas_call(
        functools.partial(group_kernel, n_dp, n_enc),
        out_shape=(
            jax.ShapeDtypeStruct((1, rows), f32),
            jax.ShapeDtypeStruct((rows, width), bf16),
            jax.ShapeDtypeStruct((slots, width), bf16),
        ),
        in_specs=[hbm, hbm, smem, smem, smem],
        out_specs=(vmem, vmem, hbm),
        scratch_shapes=[
            pltpu.VMEM((total_rows, width), bf16),
            pltpu.VMEM((passage_rows, width), bf16),
            pltpu.VMEM((n_dp, code_rows, rows), f32),
            pltpu.VMEM((n_dp, code_rows, rows), f32),
            pltpu.VMEM((passage_rows, total_rows), f32),
            pltpu.VMEM((passage_rows, total_rows), bf16),
            pltpu.VMEM((n_dp, 2, total_rows), f32),
            pltpu.VMEM((passage_rows, width), f32),
            pltpu.VMEM((slots, width), bf16),
            pltpu.VMEM((n_pair, rows, width), bf16),
            pltpu.VMEM((n_pair, rows, width), bf16),
            pltpu.VMEM((rows, width), f32),
            pltpu.VMEM((n_pair, rows, width), bf16),
            pltpu.VMEM((n_pair, rows, width), bf16),
            pltpu.VMEM((slots, passage_rows), bf16),
            dma((3,)),
            dma((2,)),
            dma((n_pair, CHUNKS)),
            dma((n_pair, CHUNKS)),
            dma((n_pair, CHUNKS)),
            dma((n_pair, CHUNKS)),
            dma((n_dp,)),
            dma((n_dp,)),
            dma((n_dp,)),
            dma((n_dp,)),
            dma((n_pair,)),
            dma((n_pair,)),
            dma((n_pair,)),
            dma((n_pair,)),
            dma((n_enc,)),
            dma((n_enc,)),
        ],
        compiler_params=pltpu.CompilerParams(
            collective_id=0, has_side_effects=True, vmem_limit_bytes=56 * 1024 * 1024
        ),
        cost_estimate=pl.CostEstimate(
            flops=6 * total_rows * passage_rows * width,
            bytes_accessed=4 * slots * width,
            transcendentals=2 * total_rows * passage_rows,
        ),
    )(queries[0], passages[0], pattern, positive, owners)
    hidden_grad = jnp.dot(received, proj_weight.T, preferred_element_type=f32).astype(bf16)
    weight_grad = jnp.dot(encoder_cache[0].T, received, preferred_element_type=f32)
    return (losses, dq[None], hidden_grad[None], weight_grad[None])


def solution(mesh):
    placed = (
        P("enc", "dp", None),
        P("enc", "dp", None),
        P("enc", "dp", None),
        P("enc", "dp"),
        P("enc", "dp", None),
        P("enc", "dp", None),
        P(),
    )
    return jax.shard_map(
        functools.partial(body, mesh.shape["dp"], mesh.shape["enc"]),
        mesh=mesh,
        in_specs=placed,
        out_specs=(
            P("enc", "dp"),
            P("enc", "dp", None),
            P("enc", "dp", None),
            P("enc", "dp", None),
        ),
        check_vma=False,
    )
```

time: 106 us -> 52.3 us (0.49)
  the two profiles are of different devices: /device:TPU:0 before, /device:TPU:15 now
where the time goes in v1:
time: 52.3 us; the launch traced here: 52.1 us
  Pallas kernels  41.9 us (80%)
  local copies, waits for them, and re-layouts  5.73 us (11%)
  matrix products  3.74 us (7%)
  between operations  0.69 us (1%)
    pallas_call x1, Pallas kernels, body(): pl.pallas_call(functools.partial(group_kernel, n_dp, n_enc), out_shape=(j...  41.9 us
    unnamed x12, local copies, waits for them, and re-layouts  5.73 us
    dot_general x1, matrix products, body(): jnp.dot(received, proj_weight.T, preferred_element_type=f32).astype(bf16)  2.94 us

profile of v1, /device:TPU:15, one launch (start us, length us, event | category | flops | bytes accessed | tf_op | source)
XLA Modules:
  0.0 52.1 jit_solution(12014012082101708108)
XLA Ops:
  0.6 0.0 copy-start
  0.6 1.4 %copy.11.owners_ref = s32[1,12,1]{2,1,0:T(8,128)} copy(s32[1,12,1]{1,2,0:T(1,128)} %param.11) | data formatting | bytes 96 | tf_op args[4]
  2.1 41.9 %shard_map.102 = (f32[1,256]{1,0:T(1,128)}, bf16[256,768]{1,0:T(8,128)(2,1)}, bf16[512,768]{1,0:T(8,128)(2,1)}) custom-call(bf16[256,768]{1,0:T(8,128)(2,1)} %bitcast.17, bf16[384,768]{1,0:T(8,128)(2,1)} %bitcast.16, s32[1,2,12]{2,1,0:T(2,128)} %pattern_ref.1, s32[1,2]{1,0:T(1,128)} %positive_ref.1, s32[1,12,1]{2,1,0:T(8,128)} %copy.11.owners_ref), custom_call_target="tpu_custom_call" | custom-call | flops 1811939328 | bytes 1572864 | tf_op jit(solution)/shard_map/pallas_call | solution.py:367
  44.0 0.0 copy-done
  44.0 0.0 copy-start.2
  44.0 0.0 copy-start.3
  44.0 2.9 %fusion = bf16[1,512,768]{2,1,0:T(8,128)(2,1)} fusion(bf16[512,768]{1,0:T(8,128)(2,1)} %get-tuple-element.9, bf16[768,768]{1,0:T(8,128)(2,1)S(1)} %copy-done), kind=kOutput, calls=%fused_computation.2 | convolution fusion | flops 604372992 | bytes 2752512 | tf_op jit(solution)/shard_map/dot_general | solution.py:418
  46.9 0.0 copy-done.2
  46.9 0.0 copy-done.3
  46.9 0.8 %convolution_bitcast_fusion = f32[1,768,768]{1,2,0:T(8,128)S(1)} fusion(bf16[512,768]{1,0:T(8,128)(2,1)S(1)} %copy-done.3, bf16[1,512,768]{2,1,0:T(8,128)(2,1)S(1)} %copy-done.2), kind=kOutput, calls=%fused_computation | convolution fusion | flops 603979776 | bytes 3932160 | tf_op jit(solution)/shard_map/dot_general | solution.py:419
  47.8 0.0 copy-start.1
  47.8 2.0 %copy.12 = f32[1,768,768]{2,1,0:T(8,128)} copy(f32[1,768,768]{1,2,0:T(8,128)S(1)} %convolution_bitcast_fusion) | data formatting | bytes 4718592
  49.7 0.0 copy-done.1
  49.7 0.6 %copy.15 = f32[1,256]{1,0:T(1,128)} copy(f32[1,256]{1,0:T(1,128)S(1)} %copy-done.1) | data formatting | bytes 2048
  50.3 1.8 %copy.16 = bf16[1,256,768]{2,1,0:T(8,128)(2,1)} copy(bf16[1,256,768]{2,1,0:T(8,128)(2,1)} %bitcast.15) | data formatting | bytes 786432
Async XLA Ops:
  0.6 43.3 %copy-start = (bf16[768,768]{1,0:T(8,128)(2,1)S(1)}, bf16[768,768]{1,0:T(8,128)(2,1)}, u32[]{:S(2)}) copy-start(bf16[768,768]{1,0:T(8,128)(2,1)} %param.13) | copy-start | bytes 3538948
  44.0 3.0 %copy-start.2 = (bf16[1,512,768]{2,1,0:T(8,128)(2,1)S(1)}, bf16[1,512,768]{2,1,0:T(8,128)(2,1)}, u32[]{:S(2)}) copy-start(bf16[1,512,768]{2,1,0:T(8,128)(2,1)} %param.12) | copy-start | bytes 2359300
  44.0 3.0 %copy-start.3 = (bf16[512,768]{1,0:T(8,128)(2,1)S(1)}, bf16[512,768]{1,0:T(8,128)(2,1)}, u32[]{:S(2)}) copy-start(bf16[512,768]{1,0:T(8,128)(2,1)} %get-tuple-element.9) | copy-start | bytes 2359300
  47.8 2.0 %copy-start.1 = (f32[1,256]{1,0:T(1,128)S(1)}, f32[1,256]{1,0:T(1,128)}, u32[]{:S(2)}) copy-start(f32[1,256]{1,0:T(1,128)} %get-tuple-element.18) | copy-start | bytes 3076

commit v2 on v1

--- a/solution.py
+++ b/solution.py
@@ -11,6 +11,7 @@
 CH = 32
 CAP = 2
 CHUNKS = 4
+LANES = 256
 NEVER = -1e30
 INVERSE_COOLNESS = 20.0
 
@@ -33,8 +34,8 @@
 def group_kernel(
     n_dp, n_enc, q_ref, p_ref, pattern_ref, positive_ref, owners_ref,
     losses_ref, dq_ref, received_ref,
-    q_all, p_own, code_out, code_all, s_all, adj, stat_all, dp_sum, outgoing,
-    dqs_out, dqs_in, dq_own, dqx_out, dqx_in, select,
+    q_all, p_own, code_out, code_all, e_all, adj, stat_all, dp_sum, outgoing,
+    dqs_out, dqs_in, dq_own, dqx_out, dqx_in, select, top_all,
     load_sem, qs_sem, qx_send, qx_recv, qf_send, qf_recv, code_send, code_recv,
     stat_send, stat_recv, dqs_send, dqs_recv, dqx_send, dqx_recv, a2a_send, a2a_recv,
 ):
@@ -124,7 +125,7 @@
         seen = jnp.int32(0)
         found = [jnp.int32(-1)] * CAP
         for c in range(span_count):
-            hit = (owners_ref[0, c, 0] == owner).astype(jnp.int32)
+            hit = (owners_ref[0, 0, c] == owner).astype(jnp.int32)
             for r in range(CAP):
                 found[r] = found[r] + (c + 1) * hit * (seen == r).astype(jnp.int32)
             seen = seen + hit
@@ -137,33 +138,35 @@
 
     lax.fori_loop(0, n_enc, select_spans, 0)
 
-    on_diagonal = (
-        lax.broadcasted_iota(jnp.int32, (BLOCK, rows), 0)
-        == lax.broadcasted_iota(jnp.int32, (BLOCK, rows), 1) % BLOCK
+    on_diagonal = lax.broadcasted_iota(jnp.int32, (BLOCK, BLOCK), 0) == lax.broadcasted_iota(
+        jnp.int32, (BLOCK, BLOCK), 1
     )
 
-    def score(source):
-        columns = rows_at(source, rows)
+    def score(source, b):
+        columns = pl.ds(pl.multiple_of(source * rows + b * BLOCK, BLOCK), BLOCK)
+        inner = pl.ds(b * BLOCK, BLOCK)
         scores = lax.dot_general(
             p_own[...], q_all[columns, :], (((1,), (1,)), ((), ())),
             preferred_element_type=jnp.float32,
         ) * INVERSE_COOLNESS
-        top = jnp.full((1, rows), NEVER, jnp.float32)
-        picked = jnp.zeros((1, rows), jnp.float32)
+        top = jnp.full((1, BLOCK), NEVER, jnp.float32)
+        picked = jnp.zeros((1, BLOCK), jnp.float32)
         masked = []
         for j in range(blocks):
             block = scores[j * BLOCK : (j + 1) * BLOCK, :]
-            code = code_all[source, j : j + 1, :]
+            code = code_all[source, j : j + 1, inner]
             block_masked = jnp.where(code > 0.5, block, NEVER)
-            s_all[j * BLOCK : (j + 1) * BLOCK, columns] = block_masked
             masked.append(block_masked)
             top = jnp.maximum(top, jnp.max(block_masked, axis=0, keepdims=True))
             hit = on_diagonal & (code > 1.5)
             picked = picked + jnp.sum(jnp.where(hit, block, 0.0), axis=0, keepdims=True)
         shift = jnp.where(top > 0.5 * NEVER, top, 0.0)
-        total = jnp.zeros((1, rows), jnp.float32)
+        total = jnp.zeros((1, BLOCK), jnp.float32)
         for j in range(blocks):
-            total = total + jnp.sum(jnp.exp(masked[j] - shift), axis=0, keepdims=True)
+            terms = jnp.exp(masked[j] - shift)
+            e_all[j * BLOCK : (j + 1) * BLOCK, columns] = terms
+            total = total + jnp.sum(terms, axis=0, keepdims=True)
+        top_all[0:1, columns] = top
         stat_all[me, 0:1, columns] = jnp.where(
             total > 0.0, shift + jnp.log(jnp.maximum(total, 1e-30)), NEVER
         )
@@ -179,30 +182,31 @@
             dp_target(source),
         ).wait_recv()
 
-    score(me)
+    for b in range(query_blocks):
+        score(me, b)
     remote(
         q_ref, q_all.at[rows_at(sibling, rows)], qs_sem.at[0], qs_sem.at[1], dp_target(sibling)
     ).wait_recv()
     for k in range(1, n_dp):
         code_wait(k)
-    score(sibling)
-
-    def take_and_forward(t, carry):
-        for h in range(CHUNKS):
-            query_arrival(t, h).wait_recv()
-            query_forward(t, h, core).start()
-        score(((pair - t + n_pair) % n_pair) * 2 + core)
+    for b in range(query_blocks):
+        score(sibling, b)
+
+    per_block = CHUNKS // query_blocks
+
+    def take(t, carry):
+        first = ((pair - t + n_pair) % n_pair) * 2
+        for b in range(query_blocks):
+            for h in range(b * per_block, (b + 1) * per_block):
+                query_arrival(t, h).wait_recv()
+                query_forward(t, h, core).start()
+            score(first + core, b)
+            for h in range(b * per_block, (b + 1) * per_block):
+                query_forward(t, h, 1 - core).wait_recv()
+            score(first + 1 - core, b)
         return carry
 
-    lax.fori_loop(1, n_pair, take_and_forward, 0)
-
-    def take_forwarded(t, carry):
-        for h in range(CHUNKS):
-            query_forward(t, h, 1 - core).wait_recv()
-        score(((pair - t + n_pair) % n_pair) * 2 + 1 - core)
-        return carry
-
-    lax.fori_loop(1, n_pair, take_forwarded, 0)
+    lax.fori_loop(1, n_pair, take, 0)
 
     def stat_copy(k, source, target):
         view = stat_all.at[source]
@@ -219,55 +223,64 @@
         top = functools.reduce(jnp.maximum, parts)
         total = functools.reduce(jnp.add, [jnp.exp(x - top) for x in parts])
         log_total = top + jnp.log(total)
+        factor = jnp.exp(top_all[0:1, columns] - log_total)
+        hit_rows = jnp.concatenate([on_diagonal] * query_blocks, axis=1)
         for j in range(blocks):
             lines = slice(j * BLOCK, (j + 1) * BLOCK)
-            hit = on_diagonal & (code_all[source, j : j + 1, :] > 1.5)
-            probability = jnp.exp(s_all[lines, columns] - log_total)
+            hit = hit_rows & (code_all[source, j : j + 1, :] > 1.5)
+            probability = e_all[lines, columns] * factor
             adj[lines, columns] = (probability - jnp.where(hit, 1.0, 0.0)).astype(jnp.bfloat16)
         return carry
 
     lax.fori_loop(0, n_dp, adjust, 0)
 
+    half = n_enc // 2
+    my_half, my_place = my_owner // half, my_owner % half
+    tiles = width // LANES
+
+    def to_owner(j, across):
+        side = (1 - my_half) if across else my_half
+        return side * half + (my_place + j) % half
+
+    def from_owner(j, across):
+        side = (1 - my_half) if across else my_half
+        return side * half + (my_place - j + half) % half
+
+    def span_copy(j, across, n, owner, place):
+        lanes = pl.ds(n * LANES, LANES)
+        sem = j + (0 if across else half)
+        return remote(
+            outgoing.at[rows_at(owner, slot_rows), lanes],
+            received_ref.at[rows_at(place, slot_rows), lanes],
+            a2a_send.at[sem, n], a2a_recv.at[sem, n], {"enc": owner},
+        )
+
     depth = min(n_dp * rows, 1024)
-    if depth == n_dp * rows:
-        for n in range(0, width, 256):
-            lanes = slice(n, n + 256)
-            dp_sum[:, lanes] = jnp.dot(
-                adj[...], q_all[:, lanes], preferred_element_type=jnp.float32
-            )
-    else:
-        dp_sum[...] = jnp.zeros_like(dp_sum)
-
-        def add_group(g, carry):
-            inner = rows_at(g, depth)
-            for n in range(0, width, 256):
-                lanes = slice(n, n + 256)
-                dp_sum[:, lanes] += jnp.dot(
+    for n in range(tiles):
+        lanes = slice(n * LANES, (n + 1) * LANES)
+        if depth == n_dp * rows:
+            total = jnp.dot(adj[...], q_all[:, lanes], preferred_element_type=jnp.float32)
+        else:
+            dp_sum[...] = jnp.zeros_like(dp_sum)
+
+            def add_group(g, carry, lanes=lanes):
+                inner = rows_at(g, depth)
+                dp_sum[...] += jnp.dot(
                     adj[:, inner], q_all[inner, lanes], preferred_element_type=jnp.float32
                 )
-            return carry
-
-        lax.fori_loop(0, n_dp * rows // depth, add_group, 0)
-
-    for n in range(0, width, 256):
-        lanes = slice(n, n + 256)
-        grad = (dp_sum[:, lanes] * INVERSE_COOLNESS).astype(jnp.bfloat16)
+                return carry
+
+            lax.fori_loop(0, n_dp * rows // depth, add_group, 0)
+            total = dp_sum[...]
+        grad = (total * INVERSE_COOLNESS).astype(jnp.bfloat16)
         outgoing[:, lanes] = jnp.dot(
             select[...], grad, preferred_element_type=jnp.float32
         ).astype(jnp.bfloat16)
-
-    def span_copy(k):
-        owner = (my_owner + k) % n_enc
-        return remote(
-            outgoing.at[rows_at(owner, slot_rows)], received_ref.at[rows_at(my_owner, slot_rows)],
-            a2a_send.at[k], a2a_recv.at[k], {"enc": owner},
-        )
-
-    def send_spans(k, carry):
-        span_copy(k).start()
-        return carry
-
-    lax.fori_loop(1, n_enc, send_spans, 0)
+        for j in range(half):
+            span_copy(j, True, n, to_owner(j, True), my_owner).start()
+            if j:
+                span_copy(j, False, n, to_owner(j, False), my_owner).start()
+
     keep = pltpu.make_async_copy(
         outgoing.at[rows_at(my_owner, slot_rows)],
         received_ref.at[rows_at(my_owner, slot_rows)],
@@ -340,22 +353,72 @@
         dqs_copy(t).wait_send()
         if t:
             dqx_copy(t).wait_send()
-    for k in range(1, n_enc):
-        span_copy(k).wait_send()
-    for k in range(1, n_enc):
-        source = (my_owner - k + n_enc) % n_enc
-        remote(
-            outgoing.at[rows_at(source, slot_rows)], received_ref.at[rows_at(source, slot_rows)],
-            a2a_send.at[k], a2a_recv.at[k], {"enc": source},
-        ).wait_recv()
+    for n in range(tiles):
+        for j in range(half):
+            for across in (True, False) if j else (True,):
+                span_copy(j, across, n, to_owner(j, across), my_owner).wait_send()
+                source = from_owner(j, across)
+                span_copy(j, across, n, source, source).wait_recv()
     keep.wait()
+
+
+def owner_kernel(
+    received_ref, cache_ref, weight_ref, losses_in, dq_in,
+    hidden_ref, grad_ref, losses_ref, dq_ref,
+    received, cache, weight, hidden, grad, in_sem, out_sem,
+):
+    loads = [
+        pltpu.make_async_copy(source, place, in_sem.at[i])
+        for i, (source, place) in enumerate(
+            [
+                (received_ref, received),
+                (cache_ref, cache),
+                (weight_ref, weight),
+                (dq_in, dq_ref),
+                (losses_in, losses_ref),
+            ]
+        )
+    ]
+    for load in loads:
+        load.start()
+    loads[0].wait()
+    loads[1].wait()
+    stores = []
+
+    def store(source, place, lines):
+        copy = pltpu.make_async_copy(
+            source.at[lines], place.at[lines], out_sem.at[len(stores)]
+        )
+        copy.start()
+        stores.append(copy)
+
+    for n in range(0, cache.shape[1], LANES):
+        lines = pl.ds(n, LANES)
+        grad[lines, :] = lax.dot_general(
+            cache[:, lines], received[...], (((0,), (0,)), ((), ())),
+            preferred_element_type=jnp.float32,
+        )
+        store(grad, grad_ref, lines)
+    loads[2].wait()
+    part = received.shape[0] // 2
+    for n in range(2):
+        lines = pl.ds(n * part, part)
+        hidden[lines, :] = lax.dot_general(
+            received[lines, :], weight[...], (((1,), (1,)), ((), ())),
+            preferred_element_type=jnp.float32,
+        ).astype(jnp.bfloat16)
+        store(hidden, hidden_ref, lines)
+    loads[3].wait()
+    loads[4].wait()
+    for copy in stores:
+        copy.wait()
 
 
 def body(n_dp, n_enc, queries, passages, pattern, positive, owners, encoder_cache, proj_weight):
     rows, width = queries.shape[1:]
     passage_rows = passages.shape[1]
     blocks = passage_rows // BLOCK
-    code_rows = -(-blocks // 8) * 8
+    code_rows = -(-blocks // 4) * 4
     n_pair = n_dp // 2
     total_rows = n_dp * rows
     slots = n_enc * CAP * CH
@@ -381,7 +444,7 @@
             pltpu.VMEM((passage_rows, total_rows), f32),
             pltpu.VMEM((passage_rows, total_rows), bf16),
             pltpu.VMEM((n_dp, 2, total_rows), f32),
-            pltpu.VMEM((passage_rows, width), f32),
+            pltpu.VMEM((passage_rows, LANES), f32),
             pltpu.VMEM((slots, width), bf16),
             pltpu.VMEM((n_pair, rows, width), bf16),
             pltpu.VMEM((n_pair, rows, width), bf16),
@@ -389,6 +452,7 @@
             pltpu.VMEM((n_pair, rows, width), bf16),
             pltpu.VMEM((n_pair, rows, width), bf16),
             pltpu.VMEM((slots, passage_rows), bf16),
+            pltpu.VMEM((1, total_rows), f32),
             dma((3,)),
             dma((2,)),
             dma((n_pair, CHUNKS)),
@@ -403,8 +467,8 @@
             dma((n_pair,)),
             dma((n_pair,)),
             dma((n_pair,)),
-            dma((n_enc,)),
-            dma((n_enc,)),
+            dma((n_enc, width // LANES)),
+            dma((n_enc, width // LANES)),
         ],
         compiler_params=pltpu.CompilerParams(
             collective_id=0, has_side_effects=True, vmem_limit_bytes=56 * 1024 * 1024
@@ -414,9 +478,34 @@
             bytes_accessed=4 * slots * width,
             transcendentals=2 * total_rows * passage_rows,
         ),
-    )(queries[0], passages[0], pattern, positive, owners)
-    hidden_grad = jnp.dot(received, proj_weight.T, preferred_element_type=f32).astype(bf16)
-    weight_grad = jnp.dot(encoder_cache[0].T, received, preferred_element_type=f32)
+    )(queries[0], passages[0], pattern, positive, owners.transpose(0, 2, 1))
+    owned, width_in = encoder_cache.shape[1:]
+    hidden_grad, weight_grad, losses, dq = pl.pallas_call(
+        owner_kernel,
+        out_shape=(
+            jax.ShapeDtypeStruct((slots, width_in), bf16),
+            jax.ShapeDtypeStruct((width_in, width), f32),
+            jax.ShapeDtypeStruct((1, rows), f32),
+            jax.ShapeDtypeStruct((rows, width), bf16),
+        ),
+        in_specs=[hbm] * 5,
+        out_specs=(hbm,) * 4,
+        scratch_shapes=[
+            pltpu.VMEM((slots, width), bf16),
+            pltpu.VMEM((owned, width_in), bf16),
+            pltpu.VMEM((width_in, width), bf16),
+            pltpu.VMEM((slots, width_in), bf16),
+            pltpu.VMEM((width_in, width), f32),
+            dma((5,)),
+            dma((width_in // LANES + 2,)),
+        ],
+        compiler_params=pltpu.CompilerParams(vmem_limit_bytes=32 * 1024 * 1024),
+        cost_estimate=pl.CostEstimate(
+            flops=4 * slots * width * width_in,
+            bytes_accessed=4 * width * width_in + 8 * slots * width,
+            transcendentals=0,
+        ),
+    )(received, encoder_cache[0], proj_weight, losses, dq)
     return (losses, dq[None], hidden_grad[None], weight_grad[None])
 
 

time: 52.3 us -> 52.2 us (level)
  the two profiles are of different devices: /device:TPU:15 before, /device:TPU:0 now
where the time goes in v2:
time: 52.2 us; the launch traced here: 52 us
  Pallas kernels  48.5 us (93%)
  local copies, waits for them, and re-layouts  2.81 us (5%)
  between operations  0.68 us (1%)
    pallas_call x1, Pallas kernels, body(): pl.pallas_call(functools.partial(group_kernel, n_dp, n_enc), out_shape=(j...  45.7 us
    pallas_call x1, Pallas kernels, body(): pl.pallas_call(owner_kernel, out_shape=(jax.ShapeDtypeStruct((slots, widt...  2.82 us
    unnamed x10, local copies, waits for them, and re-layouts  2.81 us

profile of v2, /device:TPU:0, one launch (start us, length us, event | category | flops | bytes accessed | tf_op | source)
XLA Modules:
  0.0 52.0 jit_solution(11660187918444993096)
XLA Ops:
  0.6 0.0 copy-start
  0.6 0.0 copy-start.1
  0.7 45.7 %shard_map.102 = (f32[1,256]{1,0:T(1,128)}, bf16[256,768]{1,0:T(8,128)(2,1)}, bf16[512,768]{1,0:T(8,128)(2,1)}) custom-call(bf16[256,768]{1,0:T(8,128)(2,1)} %bitcast.9, bf16[384,768]{1,0:T(8,128)(2,1)} %bitcast.8, s32[1,2,12]{2,1,0:T(2,128)} %pattern_ref.1, s32[1,2]{1,0:T(1,128)} %positive_ref.1, s32[1,1,12]{2,1,0:T(1,128)} %bitcast.10), custom_call_target="tpu_custom_call" | custom-call | flops 1811939328 | bytes 1572864 | tf_op jit(solution)/shard_map/pallas_call | solution.py:430
  46.3 0.0 copy-done
  46.3 0.0 copy-done.1
  46.3 0.0 copy-start.2
  46.4 1.1 %copy-done.2 = bf16[512,768]{1,0:T(8,128)(2,1)S(1)} copy-done((bf16[512,768]{1,0:T(8,128)(2,1)S(1)}, bf16[512,768]{1,0:T(8,128)(2,1)}, u32[]{:S(2)}) %copy-start.2) | copy-done | bytes 786456
  47.5 0.0 copy-start.3
  47.5 1.0 %copy-done.3 = bf16[256,768]{1,0:T(8,128)(2,1)S(1)} copy-done((bf16[256,768]{1,0:T(8,128)(2,1)S(1)}, bf16[256,768]{1,0:T(8,128)(2,1)}, u32[]{:S(2)}) %copy-start.3) | copy-done | bytes 393240
  48.5 0.0 copy-start.4
  48.5 0.7 %copy-done.4 = f32[1,256]{1,0:T(1,128)S(1)} copy-done((f32[1,256]{1,0:T(1,128)S(1)}, f32[1,256]{1,0:T(1,128)}, u32[]{:S(2)}) %copy-start.4) | copy-done | bytes 1048
  49.2 2.8 %shard_map.103 = (bf16[512,768]{1,0:T(8,128)(2,1)}, f32[768,768]{1,0:T(8,128)}, f32[1,256]{1,0:T(1,128)}, bf16[256,768]{1,0:T(8,128)(2,1)}) custom-call(bf16[512,768]{1,0:T(8,128)(2,1)S(1)} %copy-done.2, bf16[512,768]{1,0:T(8,128)(2,1)S(1)} %bitcast.7, bf16[768,768]{1,0:T(8,128)(2,1)S(1)} %copy-done, f32[1,256]{1,0:T(1,128)S(1)} %copy-done.4, ...), custom_call_target="tpu_custom_call" | custom-call | flops 1207959552 | bytes 5505024 | tf_op jit(solution)/shard_map/pallas_call | solution.py:483
Async XLA Ops:
  0.6 45.7 %copy-start = (bf16[768,768]{1,0:T(8,128)(2,1)S(1)}, bf16[768,768]{1,0:T(8,128)(2,1)}, u32[]{:S(2)}) copy-start(bf16[768,768]{1,0:T(8,128)(2,1)} %weight_ref.1) | copy-start | bytes 3538948
  0.6 45.7 %copy-start.1 = (bf16[1,512,768]{2,1,0:T(8,128)(2,1)S(1)}, bf16[1,512,768]{2,1,0:T(8,128)(2,1)}, u32[]{:S(2)}) copy-start(bf16[1,512,768]{2,1,0:T(8,128)(2,1)} %param.12) | copy-start | bytes 2359300
  46.3 1.1 %copy-start.2 = (bf16[512,768]{1,0:T(8,128)(2,1)S(1)}, bf16[512,768]{1,0:T(8,128)(2,1)}, u32[]{:S(2)}) copy-start(bf16[512,768]{1,0:T(8,128)(2,1)} %get-tuple-element.11.received_ref) | copy-start | bytes 2359300
  47.5 1.0 %copy-start.3 = (bf16[256,768]{1,0:T(8,128)(2,1)S(1)}, bf16[256,768]{1,0:T(8,128)(2,1)}, u32[]{:S(2)}) copy-start(bf16[256,768]{1,0:T(8,128)(2,1)} %get-tuple-element.13.dq_in) | copy-start | bytes 1179652
  48.5 0.7 %copy-start.4 = (f32[1,256]{1,0:T(1,128)S(1)}, f32[1,256]{1,0:T(1,128)}, u32[]{:S(2)}) copy-start(f32[1,256]{1,0:T(1,128)} %get-tuple-element.12.losses_in) | copy-start | bytes 3076

commit v3 on v2

--- a/solution.py
+++ b/solution.py
@@ -138,30 +138,30 @@
 
     lax.fori_loop(0, n_enc, select_spans, 0)
 
-    on_diagonal = lax.broadcasted_iota(jnp.int32, (BLOCK, BLOCK), 0) == lax.broadcasted_iota(
-        jnp.int32, (BLOCK, BLOCK), 1
+    on_diagonal = (
+        lax.broadcasted_iota(jnp.int32, (BLOCK, rows), 0)
+        == lax.broadcasted_iota(jnp.int32, (BLOCK, rows), 1) % BLOCK
     )
 
-    def score(source, b):
-        columns = pl.ds(pl.multiple_of(source * rows + b * BLOCK, BLOCK), BLOCK)
-        inner = pl.ds(b * BLOCK, BLOCK)
+    def score(source):
+        columns = rows_at(source, rows)
         scores = lax.dot_general(
             p_own[...], q_all[columns, :], (((1,), (1,)), ((), ())),
             preferred_element_type=jnp.float32,
         ) * INVERSE_COOLNESS
-        top = jnp.full((1, BLOCK), NEVER, jnp.float32)
-        picked = jnp.zeros((1, BLOCK), jnp.float32)
+        top = jnp.full((1, rows), NEVER, jnp.float32)
+        picked = jnp.zeros((1, rows), jnp.float32)
         masked = []
         for j in range(blocks):
             block = scores[j * BLOCK : (j + 1) * BLOCK, :]
-            code = code_all[source, j : j + 1, inner]
+            code = code_all[source, j : j + 1, :]
             block_masked = jnp.where(code > 0.5, block, NEVER)
             masked.append(block_masked)
             top = jnp.maximum(top, jnp.max(block_masked, axis=0, keepdims=True))
             hit = on_diagonal & (code > 1.5)
             picked = picked + jnp.sum(jnp.where(hit, block, 0.0), axis=0, keepdims=True)
         shift = jnp.where(top > 0.5 * NEVER, top, 0.0)
-        total = jnp.zeros((1, BLOCK), jnp.float32)
+        total = jnp.zeros((1, rows), jnp.float32)
         for j in range(blocks):
             terms = jnp.exp(masked[j] - shift)
             e_all[j * BLOCK : (j + 1) * BLOCK, columns] = terms
@@ -182,28 +182,23 @@
             dp_target(source),
         ).wait_recv()
 
-    for b in range(query_blocks):
-        score(me, b)
+    score(me)
     remote(
         q_ref, q_all.at[rows_at(sibling, rows)], qs_sem.at[0], qs_sem.at[1], dp_target(sibling)
     ).wait_recv()
     for k in range(1, n_dp):
         code_wait(k)
-    for b in range(query_blocks):
-        score(sibling, b)
-
-    per_block = CHUNKS // query_blocks
+    score(sibling)
 
     def take(t, carry):
         first = ((pair - t + n_pair) % n_pair) * 2
-        for b in range(query_blocks):
-            for h in range(b * per_block, (b + 1) * per_block):
-                query_arrival(t, h).wait_recv()
-                query_forward(t, h, core).start()
-            score(first + core, b)
-            for h in range(b * per_block, (b + 1) * per_block):
-                query_forward(t, h, 1 - core).wait_recv()
-            score(first + 1 - core, b)
+        for h in range(CHUNKS):
+            query_arrival(t, h).wait_recv()
+            query_forward(t, h, core).start()
+        score(first + core)
+        for h in range(CHUNKS):
+            query_forward(t, h, 1 - core).wait_recv()
+        score(first + 1 - core)
         return carry
 
     lax.fori_loop(1, n_pair, take, 0)
@@ -224,39 +219,23 @@
         total = functools.reduce(jnp.add, [jnp.exp(x - top) for x in parts])
         log_total = top + jnp.log(total)
         factor = jnp.exp(top_all[0:1, columns] - log_total)
-        hit_rows = jnp.concatenate([on_diagonal] * query_blocks, axis=1)
         for j in range(blocks):
             lines = slice(j * BLOCK, (j + 1) * BLOCK)
-            hit = hit_rows & (code_all[source, j : j + 1, :] > 1.5)
+            hit = on_diagonal & (code_all[source, j : j + 1, :] > 1.5)
             probability = e_all[lines, columns] * factor
             adj[lines, columns] = (probability - jnp.where(hit, 1.0, 0.0)).astype(jnp.bfloat16)
         return carry
 
     lax.fori_loop(0, n_dp, adjust, 0)
 
-    half = n_enc // 2
-    my_half, my_place = my_owner // half, my_owner % half
-    tiles = width // LANES
-
-    def to_owner(j, across):
-        side = (1 - my_half) if across else my_half
-        return side * half + (my_place + j) % half
-
-    def from_owner(j, across):
-        side = (1 - my_half) if across else my_half
-        return side * half + (my_place - j + half) % half
-
-    def span_copy(j, across, n, owner, place):
-        lanes = pl.ds(n * LANES, LANES)
-        sem = j + (0 if across else half)
+    def span_copy(k, owner, place):
         return remote(
-            outgoing.at[rows_at(owner, slot_rows), lanes],
-            received_ref.at[rows_at(place, slot_rows), lanes],
-            a2a_send.at[sem, n], a2a_recv.at[sem, n], {"enc": owner},
+            outgoing.at[rows_at(owner, slot_rows)], received_ref.at[rows_at(place, slot_rows)],
+            a2a_send.at[k], a2a_recv.at[k], {"enc": owner},
         )
 
     depth = min(n_dp * rows, 1024)
-    for n in range(tiles):
+    for n in range(width // LANES):
         lanes = slice(n * LANES, (n + 1) * LANES)
         if depth == n_dp * rows:
             total = jnp.dot(adj[...], q_all[:, lanes], preferred_element_type=jnp.float32)
@@ -276,11 +255,12 @@
         outgoing[:, lanes] = jnp.dot(
             select[...], grad, preferred_element_type=jnp.float32
         ).astype(jnp.bfloat16)
-        for j in range(half):
-            span_copy(j, True, n, to_owner(j, True), my_owner).start()
-            if j:
-                span_copy(j, False, n, to_owner(j, False), my_owner).start()
-
+
+    def send_spans(k, carry):
+        span_copy(k, (my_owner + k) % n_enc, my_owner).start()
+        return carry
+
+    lax.fori_loop(1, n_enc, send_spans, 0)
     keep = pltpu.make_async_copy(
         outgoing.at[rows_at(my_owner, slot_rows)],
         received_ref.at[rows_at(my_owner, slot_rows)],
@@ -353,12 +333,10 @@
         dqs_copy(t).wait_send()
         if t:
             dqx_copy(t).wait_send()
-    for n in range(tiles):
-        for j in range(half):
-            for across in (True, False) if j else (True,):
-                span_copy(j, across, n, to_owner(j, across), my_owner).wait_send()
-                source = from_owner(j, across)
-                span_copy(j, across, n, source, source).wait_recv()
+    for k in range(1, n_enc):
+        span_copy(k, (my_owner + k) % n_enc, my_owner).wait_send()
+        source = (my_owner - k + n_enc) % n_enc
+        span_copy(k, source, source).wait_recv()
     keep.wait()
 
 
@@ -467,8 +445,8 @@
             dma((n_pair,)),
             dma((n_pair,)),
             dma((n_pair,)),
-            dma((n_enc, width // LANES)),
-            dma((n_enc, width // LANES)),
+            dma((n_enc,)),
+            dma((n_enc,)),
         ],
         compiler_params=pltpu.CompilerParams(
             collective_id=0, has_side_effects=True, vmem_limit_bytes=56 * 1024 * 1024
@@ -499,7 +477,7 @@
             dma((5,)),
             dma((width_in // LANES + 2,)),
         ],
-        compiler_params=pltpu.CompilerParams(vmem_limit_bytes=32 * 1024 * 1024),
+        compiler_params=pltpu.CompilerParams(vmem_limit_bytes=56 * 1024 * 1024),
         cost_estimate=pl.CostEstimate(
             flops=4 * slots * width * width_in,
             bytes_accessed=4 * width * width_in + 8 * slots * width,

time: 52.2 us -> 56.6 us (1.084)
  the two profiles are of different devices: /device:TPU:0 before, /device:TPU:15 now
where the time goes in v3:
time: 56.6 us; the launch traced here: 56.4 us
  Pallas kernels  55.8 us (99%)
  between operations  0.64 us (1%)
    pallas_call x1, Pallas kernels, body(): pl.pallas_call(functools.partial(group_kernel, n_dp, n_enc), out_shape=(j...  42.6 us
    pallas_call x1, Pallas kernels, body(): pl.pallas_call(owner_kernel, out_shape=(jax.ShapeDtypeStruct((slots, widt...  13.1 us

profile of v3, /device:TPU:15, one launch (start us, length us, event | category | flops | bytes accessed | tf_op | source)
XLA Modules:
  0.0 56.4 jit_solution(15585932256902568202)
XLA Ops:
  0.6 42.6 %shard_map.102 = (f32[1,256]{1,0:T(1,128)}, bf16[256,768]{1,0:T(8,128)(2,1)}, bf16[512,768]{1,0:T(8,128)(2,1)}) custom-call(bf16[256,768]{1,0:T(8,128)(2,1)} %bitcast.9, bf16[384,768]{1,0:T(8,128)(2,1)} %bitcast.8, s32[1,2,12]{2,1,0:T(2,128)} %pattern_ref.1, s32[1,2]{1,0:T(1,128)} %positive_ref.1, s32[1,1,12]{2,1,0:T(1,128)} %bitcast.10), custom_call_target="tpu_custom_call" | custom-call | flops 1811939328 | bytes 1572864 | tf_op jit(solution)/shard_map/pallas_call | solution.py:408
  43.3 13.1 %shard_map.103 = (bf16[512,768]{1,0:T(8,128)(2,1)}, f32[768,768]{1,0:T(8,128)}, f32[1,256]{1,0:T(1,128)}, bf16[256,768]{1,0:T(8,128)(2,1)}) custom-call(bf16[512,768]{1,0:T(8,128)(2,1)} %get-tuple-element.11.received_ref, bf16[512,768]{1,0:T(8,128)(2,1)} %bitcast.7, bf16[768,768]{1,0:T(8,128)(2,1)} %weight_ref.1, f32[1,256]{1,0:T(1,128)} %get-tuple-element.12.losses_in, ...), custom_call_target="tpu_custom_call" | custom-call | flops 1207959552 | bytes 5505024 | tf_op jit(solution)/shard_map/pallas_call | solution.py:461

commit v4 on v3

--- a/solution.py
+++ b/solution.py
@@ -228,10 +228,21 @@
 
     lax.fori_loop(0, n_dp, adjust, 0)
 
-    def span_copy(k, owner, place):
+    half = n_enc // 2
+    my_half, my_place = my_owner // half, my_owner % half
+    turns = [(0, True)]
+    for j in range(1, half):
+        turns += [(j, False), (j, True)]
+
+    def owner_at(j, across):
+        side = (1 - my_half) if across else my_half
+        return side * half + (my_place + j + half) % half
+
+    def span_copy(j, across, owner, place):
+        sem = j if across else j + half
         return remote(
             outgoing.at[rows_at(owner, slot_rows)], received_ref.at[rows_at(place, slot_rows)],
-            a2a_send.at[k], a2a_recv.at[k], {"enc": owner},
+            a2a_send.at[sem], a2a_recv.at[sem], {"enc": owner},
         )
 
     depth = min(n_dp * rows, 1024)
@@ -256,11 +267,8 @@
             select[...], grad, preferred_element_type=jnp.float32
         ).astype(jnp.bfloat16)
 
-    def send_spans(k, carry):
-        span_copy(k, (my_owner + k) % n_enc, my_owner).start()
-        return carry
-
-    lax.fori_loop(1, n_enc, send_spans, 0)
+    for j, across in turns:
+        span_copy(j, across, owner_at(j, across), my_owner).start()
     keep = pltpu.make_async_copy(
         outgoing.at[rows_at(my_owner, slot_rows)],
         received_ref.at[rows_at(my_owner, slot_rows)],
@@ -333,17 +341,17 @@
         dqs_copy(t).wait_send()
         if t:
             dqx_copy(t).wait_send()
-    for k in range(1, n_enc):
-        span_copy(k, (my_owner + k) % n_enc, my_owner).wait_send()
-        source = (my_owner - k + n_enc) % n_enc
-        span_copy(k, source, source).wait_recv()
+    for j, across in turns:
+        span_copy(j, across, owner_at(j, across), my_owner).wait_send()
+        source = owner_at(-j, across)
+        span_copy(j, across, source, source).wait_recv()
     keep.wait()
 
 
 def owner_kernel(
     received_ref, cache_ref, weight_ref, losses_in, dq_in,
     hidden_ref, grad_ref, losses_ref, dq_ref,
-    received, cache, weight, hidden, grad, in_sem, out_sem,
+    received, cache, weight, hidden, grad, dq, losses, in_sem, out_sem,
 ):
     loads = [
         pltpu.make_async_copy(source, place, in_sem.at[i])
@@ -352,8 +360,8 @@
                 (received_ref, received),
                 (cache_ref, cache),
                 (weight_ref, weight),
-                (dq_in, dq_ref),
-                (losses_in, losses_ref),
+                (dq_in, dq),
+                (losses_in, losses),
             ]
         )
     ]
@@ -377,6 +385,10 @@
             preferred_element_type=jnp.float32,
         )
         store(grad, grad_ref, lines)
+    loads[3].wait()
+    store(dq, dq_ref, pl.ds(0, dq.shape[0]))
+    loads[4].wait()
+    store(losses, losses_ref, pl.ds(0, 1))
     loads[2].wait()
     part = received.shape[0] // 2
     for n in range(2):
@@ -386,8 +398,6 @@
             preferred_element_type=jnp.float32,
         ).astype(jnp.bfloat16)
         store(hidden, hidden_ref, lines)
-    loads[3].wait()
-    loads[4].wait()
     for copy in stores:
         copy.wait()
 
@@ -474,8 +484,10 @@
             pltpu.VMEM((width_in, width), bf16),
             pltpu.VMEM((slots, width_in), bf16),
             pltpu.VMEM((width_in, width), f32),
+            pltpu.VMEM((rows, width), bf16),
+            pltpu.VMEM((1, rows), f32),
             dma((5,)),
-            dma((width_in // LANES + 2,)),
+            dma((width_in // LANES + 4,)),
         ],
         compiler_params=pltpu.CompilerParams(vmem_limit_bytes=56 * 1024 * 1024),
         cost_estimate=pl.CostEstimate(

time: 56.6 us -> 50 us (0.88)
  the two profiles are of different devices: /device:TPU:15 before, /device:TPU:0 now
where the time goes in v4:
time: 50 us; the launch traced here: 49.8 us
  Pallas kernels  49.2 us (98%)
  between operations  0.64 us (1%)
    pallas_call x1, Pallas kernels, body(): pl.pallas_call(functools.partial(group_kernel, n_dp, n_enc), out_shape=(j...  45.3 us
    pallas_call x1, Pallas kernels, body(): pl.pallas_call(owner_kernel, out_shape=(jax.ShapeDtypeStruct((slots, widt...  3.87 us

profile of v4, /device:TPU:0, one launch (start us, length us, event | category | flops | bytes accessed | tf_op | source)
XLA Modules:
  0.0 49.8 jit_solution(15414501849372299437)
XLA Ops:
  0.6 45.3 %shard_map.102 = (f32[1,256]{1,0:T(1,128)}, bf16[256,768]{1,0:T(8,128)(2,1)}, bf16[512,768]{1,0:T(8,128)(2,1)}) custom-call(bf16[256,768]{1,0:T(8,128)(2,1)} %bitcast.9, bf16[384,768]{1,0:T(8,128)(2,1)} %bitcast.8, s32[1,2,12]{2,1,0:T(2,128)} %pattern_ref.1, s32[1,2]{1,0:T(1,128)} %positive_ref.1, s32[1,1,12]{2,1,0:T(1,128)} %bitcast.10), custom_call_target="tpu_custom_call" | custom-call | flops 1811939328 | bytes 1572864 | tf_op jit(solution)/shard_map/pallas_call | solution.py:418
  46.0 3.9 %shard_map.103 = (bf16[512,768]{1,0:T(8,128)(2,1)}, f32[768,768]{1,0:T(8,128)}, f32[1,256]{1,0:T(1,128)}, bf16[256,768]{1,0:T(8,128)(2,1)}) custom-call(bf16[512,768]{1,0:T(8,128)(2,1)} %get-tuple-element.11.received_ref, bf16[512,768]{1,0:T(8,128)(2,1)} %bitcast.7, bf16[768,768]{1,0:T(8,128)(2,1)} %weight_ref.1, f32[1,256]{1,0:T(1,128)} %get-tuple-element.12.losses_in, ...), custom_call_target="tpu_custom_call" | custom-call | flops 1207959552 | bytes 5505024 | tf_op jit(solution)/shard_map/pallas_call | solution.py:471

commit v5 on v3

--- a/solution.py
+++ b/solution.py
@@ -343,7 +343,7 @@
 def owner_kernel(
     received_ref, cache_ref, weight_ref, losses_in, dq_in,
     hidden_ref, grad_ref, losses_ref, dq_ref,
-    received, cache, weight, hidden, grad, in_sem, out_sem,
+    received, cache, weight, hidden, grad, dq, losses, in_sem, out_sem,
 ):
     loads = [
         pltpu.make_async_copy(source, place, in_sem.at[i])
@@ -352,8 +352,8 @@
                 (received_ref, received),
                 (cache_ref, cache),
                 (weight_ref, weight),
-                (dq_in, dq_ref),
-                (losses_in, losses_ref),
+                (dq_in, dq),
+                (losses_in, losses),
             ]
         )
     ]
@@ -377,6 +377,10 @@
             preferred_element_type=jnp.float32,
         )
         store(grad, grad_ref, lines)
+    loads[3].wait()
+    store(dq, dq_ref, pl.ds(0, dq.shape[0]))
+    loads[4].wait()
+    store(losses, losses_ref, pl.ds(0, 1))
     loads[2].wait()
     part = received.shape[0] // 2
     for n in range(2):
@@ -386,8 +390,6 @@
             preferred_element_type=jnp.float32,
         ).astype(jnp.bfloat16)
         store(hidden, hidden_ref, lines)
-    loads[3].wait()
-    loads[4].wait()
     for copy in stores:
         copy.wait()
 
@@ -474,8 +476,10 @@
             pltpu.VMEM((width_in, width), bf16),
             pltpu.VMEM((slots, width_in), bf16),
             pltpu.VMEM((width_in, width), f32),
+            pltpu.VMEM((rows, width), bf16),
+            pltpu.VMEM((1, rows), f32),
             dma((5,)),
-            dma((width_in // LANES + 2,)),
+            dma((width_in // LANES + 4,)),
         ],
         compiler_params=pltpu.CompilerParams(vmem_limit_bytes=56 * 1024 * 1024),
         cost_estimate=pl.CostEstimate(

time: 56.6 us -> 47.3 us (0.84)
  Pallas kernels: 55.8 us -> 46.5 us
    pallas_call x1, Pallas kernels: 13.1 us -> 3.87 us  [body(): pl.pallas_call(owner_kernel, out_shape=(jax.ShapeDtypeStruct((slots, widt...]
where the time goes in v5:
time: 47.3 us; the launch traced here: 47.2 us
  Pallas kernels  46.5 us (98%)
  between operations  0.64 us (1%)
    pallas_call x1, Pallas kernels, body(): pl.pallas_call(functools.partial(group_kernel, n_dp, n_enc), out_shape=(j...  42.6 us
    pallas_call x1, Pallas kernels, body(): pl.pallas_call(owner_kernel, out_shape=(jax.ShapeDtypeStruct((slots, widt...  3.87 us

profile of v5, /device:TPU:15, one launch (start us, length us, event | category | flops | bytes accessed | tf_op | source)
XLA Modules:
  0.0 47.2 jit_solution(1685537667662948723)
XLA Ops:
  0.6 42.6 %shard_map.102 = (f32[1,256]{1,0:T(1,128)}, bf16[256,768]{1,0:T(8,128)(2,1)}, bf16[512,768]{1,0:T(8,128)(2,1)}) custom-call(bf16[256,768]{1,0:T(8,128)(2,1)} %bitcast.9, bf16[384,768]{1,0:T(8,128)(2,1)} %bitcast.8, s32[1,2,12]{2,1,0:T(2,128)} %pattern_ref.1, s32[1,2]{1,0:T(1,128)} %positive_ref.1, s32[1,1,12]{2,1,0:T(1,128)} %bitcast.10), custom_call_target="tpu_custom_call" | custom-call | flops 1811939328 | bytes 1572864 | tf_op jit(solution)/shard_map/pallas_call | solution.py:410
  43.3 3.9 %shard_map.103 = (bf16[512,768]{1,0:T(8,128)(2,1)}, f32[768,768]{1,0:T(8,128)}, f32[1,256]{1,0:T(1,128)}, bf16[256,768]{1,0:T(8,128)(2,1)}) custom-call(bf16[512,768]{1,0:T(8,128)(2,1)} %get-tuple-element.11.received_ref, bf16[512,768]{1,0:T(8,128)(2,1)} %bitcast.7, bf16[768,768]{1,0:T(8,128)(2,1)} %weight_ref.1, f32[1,256]{1,0:T(1,128)} %get-tuple-element.12.losses_in, ...), custom_call_target="tpu_custom_call" | custom-call | flops 1207959552 | bytes 5505024 | tf_op jit(solution)/shard_map/pallas_call | solution.py:463
